TPU v7x, 32 devices: a whole 2x2x4 slice. The times are simulated.
32 devices in a mesh: rep: 4 (over x, core), fsdp: 8 (over z, y).
Axes of the slice: x: 2, y: 2, z: 4, core: 2. Of those that a mesh axis runs over, the one named last changes fastest.
Arguments:
- tokens: bfloat16 [8192, 4096], P(('rep', 'fsdp')), may hold values from -6 to 6
- cotangent: bfloat16 [8192, 512], P(('rep', 'fsdp')), may hold values from -0.0625 to 0.0625
- momentum: float32 [4, 4096, 512], P('rep', 'fsdp'), may hold values from -6 to 6
- weight: bfloat16 [4096, 512], P('fsdp'), may hold values from -0.09375 to 0.09375
- picks: int32 [4, 512, 32], P(None, 'fsdp'), may hold values from 0 to 4095, as said below
- next_tokens: bfloat16 [4096, 4096], P(('rep', 'fsdp')), may hold values from -3 to 3
Outputs:
- momentum_out: float32 [4, 4096, 512], P('rep', 'fsdp')
- next_keys: float32 [4096, 512], P(('rep', 'fsdp'))
Inputs may be any that keep to these rules, and one draw needn't show every extreme that they name: `picks`: for each replica and tile the 32 positions are distinct.
All inputs are finite; a program needn't handle non-finite values.
Results may differ from a plain program's by a relative error of at most 0.014.
Values may be sent and summed in bfloat16 or wider, within the bound.
A program may use at most 64 MiB of HBM per device.

v0:
```python
import functools
import math

import jax
import jax.numpy as jnp
import numpy as np
from jax import lax
from jax.experimental import pallas as pl
from jax.experimental.pallas import tpu as pltpu
from jax.sharding import PartitionSpec as P

TILE = 64
LANES = 2 * TILE
decay_rate = 0.999
step_size = 0.02
MESH = pl.DeviceIdType.MESH
F32 = jnp.float32
BF16 = jnp.bfloat16


def cosine_parts():
    freq = np.arange(TILE)[None, :]
    cell = np.arange(TILE)[:, None]
    table = np.cos(math.pi * (2 * cell + 1) * freq / (2 * TILE)) * math.sqrt(2 / TILE)
    table = np.where(freq == 0, table * math.sqrt(0.5), table).astype(np.float32)
    head = table.astype(BF16)
    tail = (table - head.astype(np.float32)).astype(BF16)
    return np.concatenate([head, tail, head], axis=0)


def halves(x):
    head = x.astype(BF16)
    return head, (x - head.astype(F32)).astype(BF16)


def dot_tn(a, b):
    return lax.dot_general(a, b, (((0,), (0,)), ((), ())), preferred_element_type=F32)


def dot_nt(a, b):
    return lax.dot_general(a, b, (((1,), (1,)), ((), ())), preferred_element_type=F32)


def kernel(
    n_rep, n_fsdp,
    tokens, cot, moment, weight, picks, next_tokens, table,
    moment_out, keys_out,
    own_tok, mate_tok, mate_cot, line_in, line_out, acc,
    vel, rows3, cols_hi, cols_lo, own_vals, peer_vals,
    new_weight, next_in, pair_out, pair_in, key_in, key_out,
    local_sem, cot_sems, tok_send, tok_recv, line_send, line_recv,
    val_send, val_recv, next_send, next_recv, pair_send, pair_recv,
    key_send, key_recv,
):
    groups = n_fsdp // 2
    rep = lax.axis_index("rep")
    me = lax.axis_index("fsdp")
    side = lax.rem(me, 2)
    place = me // 2
    mate = me + 1 - 2 * side
    rows, cols = weight.shape
    pairs, width = picks.shape
    per_tile = width // 2
    kept = per_tile // n_rep
    across = cols // LANES

    barrier = pltpu.get_barrier_semaphore()
    for step in range(1, n_fsdp):
        pl.semaphore_signal(
            barrier, inc=1, device_id={"fsdp": lax.rem(me + step, n_fsdp)}, device_id_type=MESH
        )
    for step in range(1, n_rep):
        pl.semaphore_signal(
            barrier, inc=1, device_id={"rep": lax.rem(rep + step, n_rep)}, device_id_type=MESH
        )
    pl.semaphore_wait(barrier, n_fsdp + n_rep - 2)

    def block(owner):
        return pl.ds(pl.multiple_of(owner * rows, rows), rows)

    def remote(src, dst, send, recv, **device):
        return pltpu.make_async_remote_copy(
            src_ref=src, dst_ref=dst, send_sem=send, recv_sem=recv,
            device_id=device, device_id_type=MESH,
        )

    def each_event(body):
        def step(event, carry):
            way = lax.rem(event, 2)
            turn = event // 2
            group = way * turn + (1 - way) * (groups - 1 - turn)
            active = ((way == 0) & (place < group)) | ((way == 1) & (place > group))

            @pl.when(active)
            def _():
                body(way, group)

            return carry

        lax.fori_loop(0, 2 * (groups - 1), step, 0)

    def cot_copy():
        return remote(cot, mate_cot, cot_sems.at[0], cot_sems.at[1], fsdp=mate)

    def tok_copy(group):
        return remote(
            tokens.at[:, block(2 * group + 1 - side)], mate_tok.at[group],
            tok_send.at[group], tok_recv.at[group], fsdp=mate,
        )

    def tok_local(group):
        return pltpu.make_async_copy(
            tokens.at[:, block(2 * group + side)], own_tok.at[group], local_sem.at[group]
        )

    def next_copy(step):
        target = lax.rem(me + step, n_fsdp)
        return remote(
            next_tokens.at[:, block(target)], next_in.at[me],
            next_send.at[step], next_recv.at[me], fsdp=target,
        )

    def next_wait(source):
        return remote(
            next_tokens.at[:, block(me)], next_in.at[source],
            next_send.at[0], next_recv.at[source], fsdp=mate,
        )

    def next_local():
        return pltpu.make_async_copy(
            next_tokens.at[:, block(me)], next_in.at[me], local_sem.at[groups]
        )

    cot_copy().start()
    each_event(lambda way, group: tok_copy(group).start())
    tok_copy(place).start()
    each_event(lambda way, group: tok_local(group).start())
    tok_local(place).start()
    next_local().start()
    for step in range(1, n_fsdp):
        next_copy(step).start()

    def name_rows(pair, carry):
        spots = picks[pl.ds(pair, 1), :]
        ids = lax.broadcasted_iota(jnp.int32, (TILE, width), 0)
        pick_row = jnp.where(ids == spots // TILE, 1.0, 0.0).astype(BF16)
        pick_col = jnp.where(ids == lax.rem(spots, TILE), 1.0, 0.0).astype(BF16)
        rows3[pair] = jnp.dot(table[...], pick_row, preferred_element_type=F32).astype(BF16)
        found = jnp.dot(
            table[pl.ds(0, LANES), :], pick_col, preferred_element_type=F32
        )
        first = lax.broadcasted_iota(jnp.int32, (TILE, width), 1) < per_tile
        for part, target in ((found[:TILE], cols_hi), (found[TILE:], cols_lo)):
            target[pair] = jnp.concatenate(
                [jnp.where(first, part, 0.0), jnp.where(first, 0.0, part)], axis=0
            ).astype(BF16)
        return carry

    lax.fori_loop(0, pairs, name_rows, 0)

    def line_copy(way, group, source, target, send, recv):
        return remote(
            source.at[group], target.at[way, group], send.at[group], recv.at[way, group],
            fsdp=lax.rem(me + 2 - 4 * way + n_fsdp, n_fsdp),
        )

    def line_reduce(term, total, source, target, send, recv):
        def take(way, group):
            line_copy(way, group, source, target, send, recv).wait_recv()
            total[...] += target[way, group].astype(F32)

        def handle(way, group):
            total[...] = term(group)

            @pl.when(((way == 0) & (place > 0)) | ((way == 1) & (place < groups - 1)))
            def _():
                take(way, group)

            source[group] = total[...].astype(BF16)
            line_copy(way, group, source, target, send, recv).start()

        each_event(handle)
        total[...] = term(place)

        @pl.when(place > 0)
        def _():
            take(0, place)

        @pl.when(place < groups - 1)
        def _():
            take(1, place)

    cot_copy().wait_recv()

    def grad_term(group):
        tok_local(group).wait()
        tok_copy(group).wait_recv()
        return dot_tn(own_tok[group], cot[...]) + dot_tn(mate_tok[group], mate_cot[...])

    line_reduce(grad_term, acc, line_out, line_in, line_send, line_recv)
    vel[...] = decay_rate * moment[0] + acc[...]

    def window(pair):
        top = pl.multiple_of(pair // across * TILE, TILE)
        left = pl.multiple_of(lax.rem(pair, across) * LANES, LANES)
        return pl.ds(top, TILE), pl.ds(left, LANES)

    def coefficients(pair, carry):
        down, over = window(pair)
        head, tail = halves(vel[down, over])
        half = dot_tn(jnp.concatenate([head, head, tail], axis=0), rows3[pair])
        full = cols_hi[pair].astype(F32) + cols_lo[pair].astype(F32)
        found = jnp.sum(half * full, axis=0, keepdims=True)
        lane = lax.broadcasted_iota(jnp.int32, (1, width), 1)
        mine = lax.rem(lane, per_tile) // kept == rep
        own_vals[pl.ds(pair, 1), :] = jnp.where(mine, found, 0.0)
        return carry

    lax.fori_loop(0, pairs, coefficients, 0, unroll=4)

    def val_copy(step):
        return remote(
            own_vals, peer_vals.at[step - 1], val_send.at[step], val_recv.at[step],
            rep=lax.rem(rep + step, n_rep),
        )

    for step in range(1, n_rep):
        val_copy(step).start()

    def inverse(pair, values):
        row_parts = rows3[pair]
        scaled = (row_parts[:TILE].astype(F32) + row_parts[TILE:LANES].astype(F32)) * values
        head, tail = halves(scaled)
        both = dot_nt(jnp.concatenate([head, tail], axis=0), cols_hi[pair])
        return both[:TILE] + both[TILE:] + dot_nt(head, cols_lo[pair])

    def residual(pair, carry):
        down, over = window(pair)
        moment_out[0, down, over] = vel[down, over] - inverse(pair, own_vals[pl.ds(pair, 1), :])
        return carry

    lax.fori_loop(0, pairs, residual, 0, unroll=4)

    for step in range(1, n_rep):
        val_copy(step).wait_recv()

    def renew(pair, carry):
        down, over = window(pair)
        values = own_vals[pl.ds(pair, 1), :]
        for step in range(1, n_rep):
            values += peer_vals[step - 1, pl.ds(pair, 1), :]
        new_weight[down, over] = (
            weight[down, over].astype(F32) - step_size * inverse(pair, values)
        ).astype(BF16)
        return carry

    lax.fori_loop(0, pairs, renew, 0, unroll=4)

    next_local().wait()
    for step in range(1, n_fsdp):
        next_wait(lax.rem(me + n_fsdp - step, n_fsdp)).wait_recv()

    def key_part(owner):
        return jnp.dot(next_in[owner], new_weight[...], preferred_element_type=F32)

    def pair_copy(group):
        return remote(
            pair_out.at[group], pair_in.at[group],
            pair_send.at[group], pair_recv.at[group], fsdp=mate,
        )

    def send_pair(group):
        pair_out[group] = key_part(2 * group + 1 - side).astype(BF16)
        pair_copy(group).start()

    each_event(lambda way, group: send_pair(group))
    send_pair(place)

    def key_term(group):
        own = key_part(2 * group + side)
        pair_copy(group).wait_recv()
        return own + pair_in[group].astype(F32)

    line_reduce(key_term, keys_out, key_out, key_in, key_send, key_recv)

    cot_copy().wait_send()
    for step in range(1, n_fsdp):
        next_copy(step).wait_send()
    for step in range(1, n_rep):
        val_copy(step).wait_send()

    def finish(way, group):
        tok_copy(group).wait_send()
        pair_copy(group).wait_send()
        line_copy(way, group, line_out, line_in, line_send, line_recv).wait_send()
        line_copy(way, group, key_out, key_in, key_send, key_recv).wait_send()

    each_event(finish)
    tok_copy(place).wait_send()
    pair_copy(place).wait_send()


def on_device(n_rep, n_fsdp, tokens, cotangent, momentum, weight, picks, next_tokens):
    groups = n_fsdp // 2
    rows, cols = weight.shape
    count = tokens.shape[0]
    ahead = next_tokens.shape[0]
    tiles, kept = picks.shape[1:]
    pairs, width = tiles // 2, 2 * n_rep * kept
    spots = jnp.transpose(picks, (1, 0, 2)).reshape(pairs, width)
    dma = pltpu.SemaphoreType.DMA
    vmem = pl.BlockSpec(memory_space=pltpu.VMEM)
    hbm = pl.BlockSpec(memory_space=pl.ANY)
    return pl.pallas_call(
        functools.partial(kernel, n_rep, n_fsdp),
        out_shape=(
            jax.ShapeDtypeStruct(momentum.shape, F32),
            jax.ShapeDtypeStruct((ahead, cols), F32),
        ),
        in_specs=[hbm, vmem, vmem, vmem, vmem, hbm, vmem],
        out_specs=(vmem, vmem),
        scratch_shapes=[
            pltpu.VMEM((groups, count, rows), BF16),
            pltpu.VMEM((groups, count, rows), BF16),
            pltpu.VMEM((count, cols), BF16),
            pltpu.VMEM((2, groups, rows, cols), BF16),
            pltpu.VMEM((groups, rows, cols), BF16),
            pltpu.VMEM((rows, cols), F32),
            pltpu.VMEM((rows, cols), F32),
            pltpu.VMEM((pairs, 3 * TILE, width), BF16),
            pltpu.VMEM((pairs, LANES, width), BF16),
            pltpu.VMEM((pairs, LANES, width), BF16),
            pltpu.VMEM((pairs, width), F32),
            pltpu.VMEM((n_rep - 1, pairs, width), F32),
            pltpu.VMEM((rows, cols), BF16),
            pltpu.VMEM((n_fsdp, ahead, rows), BF16),
            pltpu.VMEM((groups, ahead, cols), BF16),
            pltpu.VMEM((groups, ahead, cols), BF16),
            pltpu.VMEM((2, groups, ahead, cols), BF16),
            pltpu.VMEM((groups, ahead, cols), BF16),
            dma((groups + 1,)),
            dma((2,)),
            dma((groups,)),
            dma((groups,)),
            dma((groups,)),
            dma((2, groups)),
            dma((n_rep,)),
            dma((n_rep,)),
            dma((n_fsdp,)),
            dma((n_fsdp,)),
            dma((groups,)),
            dma((groups,)),
            dma((groups,)),
            dma((2, groups)),
        ],
        compiler_params=pltpu.CompilerParams(
            collective_id=0, has_side_effects=True, vmem_limit_bytes=52 * 1024 * 1024
        ),
    )(tokens, cotangent, momentum, weight, spots, next_tokens, jnp.asarray(cosine_parts()))


def solution(mesh):
    placed = (
        P(("rep", "fsdp"), None),
        P(("rep", "fsdp"), None),
        P("rep", "fsdp", None),
        P("fsdp", None),
        P(None, "fsdp", None),
        P(("rep", "fsdp"), None),
    )
    return jax.shard_map(
        functools.partial(on_device, mesh.shape["rep"], mesh.shape["fsdp"]),
        mesh=mesh,
        in_specs=placed,
        out_specs=(P("rep", "fsdp", None), P(("rep", "fsdp"), None)),
        check_vma=False,
    )
```

profile of v0, /device:TPU:0, one launch (start us, length us, event | category | flops | bytes accessed | tf_op | source)
XLA Modules:
  0.0 113.5 jit_solution(10211626657084081119)
XLA Ops:
  0.6 0.9 copy.10
  1.6 0.1 reshape.7.picks
  1.7 0.0 copy-start
  1.7 1.0 copy-done
  2.8 0.0 copy-start.1
  2.8 0.9 copy-done.1
  3.7 0.0 copy-start.2
  3.7 0.8 copy-done.2
  4.5 106.0 %shard_map.86 = (f32[1,512,512]{2,1,0:T(8,128)}, f32[128,512]{1,0:T(8,128)S(1)}) custom-call(bf16[256,4096]{1,0:T(8,128)(2,1)} %tokens.1, bf16[256,512]{1,0:T(8,128)(2,1)S(1)} %copy-done.1, f32[1,512,512]{2,1,0:T(8,128)} %moment.1, bf16[512,512]{1,0:T(8,128)(2,1)S(1)} %copy-done, s32[32,256]{1,0:T(8,128)S(1)} %reshape.7.picks, ...), custom_call_target="tpu_custom_call" | custom-call | tf_op jit(solution)/shard_map/pallas_call | solution.py:314
  110.5 2.3 %copy.13 = f32[1,512,512]{2,1,0:T(8,128)} copy(f32[1,512,512]{2,1,0:T(8,128)} %get-tuple-element.4) | data formatting | bytes 2097152
  112.8 0.7 copy.14
Async XLA Ops:
  1.7 1.0 copy-start
  2.8 0.9 copy-start.1
  3.7 0.8 copy-start.2
where the time goes:
time: 115 us; the launch traced here: 114 us
  Pallas kernels  106 us (92%)
  local copies, waits for them, and re-layouts  6.82 us (6%)
    pallas_call x1, Pallas kernels, on_device(): pl.pallas_call(functools.partial(kernel, n_rep, n_fsdp), out_shape=(jax.S...  106 us
    unnamed x8, local copies, waits for them, and re-layouts  5.75 us

commit v1 on v0

v1 whole, which is shorter than its diff:
```python
import functools
import math

import jax
import jax.numpy as jnp
import numpy as np
from jax import lax
from jax.experimental import pallas as pl
from jax.experimental.pallas import tpu as pltpu
from jax.sharding import PartitionSpec as P

TILE = 64
LANES = 2 * TILE
decay_rate = 0.999
step_size = 0.02
MESH = pl.DeviceIdType.MESH
F32 = jnp.float32
BF16 = jnp.bfloat16


def cosine_parts():
    freq = np.arange(TILE)[None, :]
    cell = np.arange(TILE)[:, None]
    table = np.cos(math.pi * (2 * cell + 1) * freq / (2 * TILE)) * math.sqrt(2 / TILE)
    table = np.where(freq == 0, table * math.sqrt(0.5), table).astype(np.float32)
    head = table.astype(BF16)
    tail = (table - head.astype(np.float32)).astype(BF16)
    return np.concatenate([head, tail, head], axis=0)


def halves(x):
    head = x.astype(BF16)
    return head, (x - head.astype(F32)).astype(BF16)


def dot_tn(a, b):
    return lax.dot_general(a, b, (((0,), (0,)), ((), ())), preferred_element_type=F32)


def dot_nt(a, b):
    return lax.dot_general(a, b, (((1,), (1,)), ((), ())), preferred_element_type=F32)


def kernel(
    n_rep, n_fsdp,
    tokens, cot_far, moment_far, weight_far, picks, next_tokens, table,
    moment_out, keys_out,
    cot, moment, weight, own_tok, mate_tok, mate_cot, line_in, line_out, acc,
    vel, rows3, cols_hi, cols_lo, own_vals, peer_vals,
    new_weight, next_in, key_in, key_out,
    near_sem, local_sem, cot_sems, tok_send, tok_recv, line_send, line_recv,
    val_send, val_recv, next_send, next_recv, half_send, half_recv,
    key_send, key_recv,
):
    groups = n_fsdp // 2
    rep = lax.axis_index("rep")
    me = lax.axis_index("fsdp")
    side = lax.rem(me, 2)
    place = me // 2
    mate = me + 1 - 2 * side
    core = lax.rem(rep, 2)
    sibling = rep + 1 - 2 * core
    rows, cols = weight.shape
    kept = picks.shape[2]
    pairs, width = own_vals.shape
    per_tile = width // 2
    across = cols // LANES
    half = rows // 2

    near = [
        pltpu.make_async_copy(far, here, near_sem.at[at])
        for at, (far, here) in enumerate(
            ((cot_far, cot), (moment_far.at[0], moment), (weight_far, weight))
        )
    ]
    for copy in near:
        copy.start()

    def peer(step):
        return 2 * lax.rem(place + step, groups) + side

    barrier = pltpu.get_barrier_semaphore()
    pl.semaphore_signal(barrier, inc=1, device_id={"fsdp": mate}, device_id_type=MESH)
    for step in range(1, groups):
        pl.semaphore_signal(barrier, inc=1, device_id={"fsdp": peer(step)}, device_id_type=MESH)
    for step in range(1, n_rep):
        pl.semaphore_signal(
            barrier, inc=1, device_id={"rep": lax.rem(rep + step, n_rep)}, device_id_type=MESH
        )
    pl.semaphore_wait(barrier, groups + n_rep - 1)

    def block(owner):
        return pl.ds(pl.multiple_of(owner * rows, rows), rows)

    def remote(src, dst, send, recv, **device):
        return pltpu.make_async_remote_copy(
            src_ref=src, dst_ref=dst, send_sem=send, recv_sem=recv,
            device_id=device, device_id_type=MESH,
        )

    above, below = groups - 1 - place, place
    both_ways = jnp.minimum(above, below)

    def order(at):
        way = jnp.where(at < 2 * both_ways, lax.rem(at, 2), jnp.where(above > below, 0, 1))
        turn = jnp.where(at < 2 * both_ways, at // 2, at - both_ways)
        group = jnp.where(way == 0, groups - 1 - turn, turn)
        return way, jnp.where(at == groups - 1, place, group)

    def cot_copy():
        return remote(cot_far, mate_cot, cot_sems.at[0], cot_sems.at[1], fsdp=mate)

    def tok_copy(group):
        return remote(
            tokens.at[:, block(2 * group + 1 - side)], mate_tok.at[group],
            tok_send.at[group], tok_recv.at[group], fsdp=mate,
        )

    def tok_local(group):
        return pltpu.make_async_copy(
            tokens.at[:, block(2 * group + side)], own_tok.at[group], local_sem.at[group]
        )

    def wide(group):
        return pl.ds(pl.multiple_of(group * 2 * rows, 2 * rows), 2 * rows)

    def next_copy(step):
        group = lax.rem(place + step, groups)
        return remote(
            next_tokens.at[:, wide(group)], next_in.at[place],
            next_send.at[step], next_recv.at[place], fsdp=2 * group + side,
        )

    def next_wait(step):
        source = lax.rem(place + groups - step, groups)
        return remote(
            next_tokens.at[:, wide(place)], next_in.at[source],
            next_send.at[step], next_recv.at[source], fsdp=mate,
        )

    def next_local():
        return pltpu.make_async_copy(
            next_tokens.at[:, wide(place)], next_in.at[place], local_sem.at[groups]
        )

    cot_copy().start()
    tok_copy(order(0)[1]).start()
    for step in range(1, groups):
        next_copy(step).start()
    for group in range(groups):
        tok_local(group).start()
    next_local().start()

    def name_rows(pair, carry):
        spots = jnp.concatenate(
            [picks[at, pl.ds(2 * pair + t, 1), :] for t in range(2) for at in range(n_rep)], axis=1
        )
        ids = lax.broadcasted_iota(jnp.int32, (TILE, width), 0)
        pick_row = jnp.where(ids == spots // TILE, 1.0, 0.0).astype(BF16)
        pick_col = jnp.where(ids == lax.rem(spots, TILE), 1.0, 0.0).astype(BF16)
        rows3[pair] = jnp.dot(table[...], pick_row, preferred_element_type=F32).astype(BF16)
        found = jnp.dot(
            table[pl.ds(0, LANES), :], pick_col, preferred_element_type=F32
        )
        first = lax.broadcasted_iota(jnp.int32, (TILE, width), 1) < per_tile
        for part, target in ((found[:TILE], cols_hi), (found[TILE:], cols_lo)):
            target[pair] = jnp.concatenate(
                [jnp.where(first, part, 0.0), jnp.where(first, 0.0, part)], axis=0
            ).astype(BF16)
        return carry

    lax.fori_loop(0, pairs, name_rows, 0, unroll=2)

    def line_copy(way, group, source, target, send, recv):
        return remote(
            source.at[group], target.at[way, group], send.at[group], recv.at[way, group],
            fsdp=lax.rem(me + 2 - 4 * way + n_fsdp, n_fsdp),
        )

    def line_reduce(term, total, source, target, send, recv):
        def copy(way, group):
            return line_copy(way, group, source, target, send, recv)

        def take(way, group):
            copy(way, group).wait_recv()
            total[...] += target[way, group].astype(F32)

        def handle(at, carry):
            way, group = order(at)
            total[...] = term(group, at)

            @pl.when(((way == 0) & (place > 0)) | ((way == 1) & (place < groups - 1)))
            def _():
                take(way, group)

            source[group] = total[...].astype(BF16)

            @pl.when(((way == 0) & (group < groups - 1)) | ((way == 1) & (group > 0)))
            def _():
                copy(way, group + 1 - 2 * way).wait_send()

            copy(way, group).start()
            return carry

        lax.fori_loop(0, groups - 1, handle, 0)
        total[...] = term(place, None)

        @pl.when(place > 0)
        def _():
            take(0, place)

        @pl.when(place < groups - 1)
        def _():
            take(1, place)

    def line_finish(source, target, send, recv):
        @pl.when(place < groups - 1)
        def _():
            line_copy(0, place + 1, source, target, send, recv).wait_send()

        @pl.when(place > 0)
        def _():
            line_copy(1, place - 1, source, target, send, recv).wait_send()

    near[0].wait()
    cot_copy().wait_recv()

    def grad_term(group, at):
        tok_local(group).wait()
        tok_copy(group).wait_recv()
        tok_copy(group).wait_send()
        if at is not None:
            tok_copy(order(at + 1)[1]).start()
        return dot_tn(own_tok[group], cot[...]) + dot_tn(mate_tok[group], mate_cot[...])

    line_reduce(grad_term, acc, line_out, line_in, line_send, line_recv)
    for step in range(0):
        next_copy(step).start()
    near[1].wait()
    vel[...] = decay_rate * moment[...] + acc[...]

    def window(pair):
        top = pl.multiple_of(pair // across * TILE, TILE)
        left = pl.multiple_of(lax.rem(pair, across) * LANES, LANES)
        return pl.ds(top, TILE), pl.ds(left, LANES)

    def coefficients(pair, carry):
        down, over = window(pair)
        head, tail = halves(vel[down, over])
        partly = dot_tn(jnp.concatenate([head, head, tail], axis=0), rows3[pair])
        full = cols_hi[pair].astype(F32) + cols_lo[pair].astype(F32)
        found = jnp.sum(partly * full, axis=0, keepdims=True)
        lane = lax.broadcasted_iota(jnp.int32, (1, width), 1)
        mine = lax.rem(lane, per_tile) // kept == rep
        own_vals[pl.ds(pair, 1), :] = jnp.where(mine, found, 0.0)
        return carry

    lax.fori_loop(0, pairs, coefficients, 0, unroll=8)

    def val_copy(step):
        return remote(
            own_vals, peer_vals.at[step - 1], val_send.at[step], val_recv.at[step],
            rep=lax.rem(rep + step, n_rep),
        )

    for step in range(1, n_rep):
        val_copy(step).start()

    def inverse(pair, values):
        row_parts = rows3[pair]
        scaled = (row_parts[:TILE].astype(F32) + row_parts[TILE:LANES].astype(F32)) * values
        head, tail = halves(scaled)
        both = dot_nt(jnp.concatenate([head, tail], axis=0), cols_hi[pair])
        return both[:TILE] + both[TILE:] + dot_nt(head, cols_lo[pair])

    def residual(pair, carry):
        down, over = window(pair)
        moment_out[0, down, over] = vel[down, over] - inverse(pair, own_vals[pl.ds(pair, 1), :])
        return carry

    lax.fori_loop(0, pairs // 2, residual, 0, unroll=8)

    near[2].wait()
    for step in range(1, n_rep):
        val_copy(step).wait_recv()

    def renew_half(which):
        def renew(at, carry):
            pair = which * (pairs // 2) + at
            down, over = window(pair)
            values = own_vals[pl.ds(pair, 1), :]
            for step in range(1, n_rep):
                values += peer_vals[step - 1, pl.ds(pair, 1), :]
            new_weight[side, down, over] = (
                weight[down, over].astype(F32) - step_size * inverse(pair, values)
            ).astype(BF16)
            return carry

        lax.fori_loop(0, pairs // 2, renew, 0, unroll=8)

    def half_rows(owner_side, which):
        return new_weight.at[owner_side, pl.ds(pl.multiple_of(which * half, half), half)]

    def half_copy():
        return remote(
            half_rows(side, core), half_rows(side, core),
            half_send.at[0], half_recv.at[0], fsdp=mate,
        )

    def half_wait():
        return remote(
            half_rows(1 - side, core), half_rows(1 - side, core),
            half_send.at[0], half_recv.at[0], fsdp=mate,
        )

    def pass_copy():
        return remote(
            half_rows(1 - side, core), half_rows(1 - side, core),
            half_send.at[1], half_recv.at[1], rep=sibling,
        )

    def pass_wait():
        return remote(
            half_rows(1 - side, 1 - core), half_rows(1 - side, 1 - core),
            half_send.at[1], half_recv.at[1], rep=sibling,
        )

    renew_half(core)
    half_copy().start()
    renew_half(1 - core)
    lax.fori_loop(pairs // 2, pairs, residual, 0, unroll=8)
    half_wait().wait_recv()
    pass_copy().start()
    next_local().wait()
    for step in range(1, groups):
        next_wait(step).wait_recv()
    pass_wait().wait_recv()

    def key_term(group, at):
        return jnp.dot(
            next_in[group, :, pl.ds(0, rows)], new_weight[0], preferred_element_type=F32
        ) + jnp.dot(
            next_in[group, :, pl.ds(rows, rows)], new_weight[1], preferred_element_type=F32
        )

    line_reduce(key_term, keys_out, key_out, key_in, key_send, key_recv)

    cot_copy().wait_send()
    for step in range(1, groups):
        next_copy(step).wait_send()
    for step in range(1, n_rep):
        val_copy(step).wait_send()
    half_copy().wait_send()
    pass_copy().wait_send()
    line_finish(line_out, line_in, line_send, line_recv)
    line_finish(key_out, key_in, key_send, key_recv)


def on_device(n_rep, n_fsdp, tokens, cotangent, momentum, weight, picks, next_tokens):
    groups = n_fsdp // 2
    rows, cols = weight.shape
    count = tokens.shape[0]
    ahead = next_tokens.shape[0]
    tiles, kept = picks.shape[1:]
    pairs, width = tiles // 2, 2 * n_rep * kept
    dma = pltpu.SemaphoreType.DMA
    vmem = pl.BlockSpec(memory_space=pltpu.VMEM)
    hbm = pl.BlockSpec(memory_space=pl.ANY)
    return pl.pallas_call(
        functools.partial(kernel, n_rep, n_fsdp),
        out_shape=(
            jax.ShapeDtypeStruct(momentum.shape, F32),
            jax.ShapeDtypeStruct((ahead, cols), F32),
        ),
        in_specs=[hbm, hbm, hbm, hbm, vmem, hbm, vmem],
        out_specs=(vmem, vmem),
        scratch_shapes=[
            pltpu.VMEM((count, cols), BF16),
            pltpu.VMEM((rows, cols), F32),
            pltpu.VMEM((rows, cols), BF16),
            pltpu.VMEM((groups, count, rows), BF16),
            pltpu.VMEM((groups, count, rows), BF16),
            pltpu.VMEM((count, cols), BF16),
            pltpu.VMEM((2, groups, rows, cols), BF16),
            pltpu.VMEM((groups, rows, cols), BF16),
            pltpu.VMEM((rows, cols), F32),
            pltpu.VMEM((rows, cols), F32),
            pltpu.VMEM((pairs, 3 * TILE, width), BF16),
            pltpu.VMEM((pairs, LANES, width), BF16),
            pltpu.VMEM((pairs, LANES, width), BF16),
            pltpu.VMEM((pairs, width), F32),
            pltpu.VMEM((n_rep - 1, pairs, width), F32),
            pltpu.VMEM((2, rows, cols), BF16),
            pltpu.VMEM((groups, ahead, 2 * rows), BF16),
            pltpu.VMEM((2, groups, ahead, cols), BF16),
            pltpu.VMEM((groups, ahead, cols), BF16),
            dma((3,)),
            dma((groups + 1,)),
            dma((2,)),
            dma((groups,)),
            dma((groups,)),
            dma((groups,)),
            dma((2, groups)),
            dma((n_rep,)),
            dma((n_rep,)),
            dma((groups,)),
            dma((groups,)),
            dma((2,)),
            dma((2,)),
            dma((groups,)),
            dma((2, groups)),
        ],
        compiler_params=pltpu.CompilerParams(
            collective_id=0, has_side_effects=True, vmem_limit_bytes=52 * 1024 * 1024
        ),
    )(tokens, cotangent, momentum, weight, picks, next_tokens, jnp.asarray(cosine_parts()))


def solution(mesh):
    placed = (
        P(("rep", "fsdp"), None),
        P(("rep", "fsdp"), None),
        P("rep", "fsdp", None),
        P("fsdp", None),
        P(None, "fsdp", None),
        P(("rep", "fsdp"), None),
    )
    return jax.shard_map(
        functools.partial(on_device, mesh.shape["rep"], mesh.shape["fsdp"]),
        mesh=mesh,
        in_specs=placed,
        out_specs=(P("rep", "fsdp", None), P(("rep", "fsdp"), None)),
        check_vma=False,
    )
```

time: 115 us -> 113 us (0.983); the launches traced: 114 us -> 113 us
    unnamed x8 -> x9, local copies, waits for them, and re-layouts: 5.75 us -> 6.68 us
where the time goes in v1:
time: 113 us
  Pallas kernels  106 us (94%)
  local copies, waits for them, and re-layouts  6.68 us (6%)
    pallas_call x1, Pallas kernels, on_device(): pl.pallas_call(functools.partial(kernel, n_rep, n_fsdp), out_shape=(jax.S...  106 us
    unnamed x9, local copies, waits for them, and re-layouts  6.68 us

profile of v1, /device:TPU:0, one launch (start us, length us, event | category | flops | bytes accessed | tf_op | source)
XLA Modules:
  0.0 112.9 jit_solution(4104581584753867614)
XLA Ops:
  0.6 0.9 copy.9.picks
  1.6 0.0 copy-start
  1.6 1.0 copy-done
  2.6 0.0 copy-start.1
  2.6 0.9 copy-done.1
  3.6 0.0 copy-start.2
  3.6 0.8 copy-done.2
  4.4 105.5 %shard_map.86 = (f32[1,512,512]{2,1,0:T(8,128)}, f32[128,512]{1,0:T(8,128)S(1)}) custom-call(bf16[256,4096]{1,0:T(8,128)(2,1)} %tokens.1, bf16[256,512]{1,0:T(8,128)(2,1)S(1)} %copy-done.1, f32[1,512,512]{2,1,0:T(8,128)} %moment_far.1, bf16[512,512]{1,0:T(8,128)(2,1)S(1)} %copy-done, s32[4,64,32]{2,1,0:T(8,128)S(1)} %copy.9.picks, ...), custom_call_target="tpu_custom_call" | custom-call | tf_op jit(solution)/shard_map/pallas_call | solution.py:369
  109.9 2.3 %copy.12 = f32[1,512,512]{2,1,0:T(8,128)} copy(f32[1,512,512]{2,1,0:T(8,128)} %get-tuple-element.4) | data formatting | bytes 2097152
  112.2 0.7 copy.13
Async XLA Ops:
  1.6 1.0 copy-start
  2.6 0.9 copy-start.1
  3.6 0.8 copy-start.2
